TPU v7x, 128 devices: a whole 4x4x4 slice. The times are simulated.
128 devices in a mesh: row: 32 (over x_lo, z, y), col: 4 (over x_hi, core).
Axes of the slice: x: 4 (x_hi: 2, x_lo: 2; x = x_hi * 2 + x_lo), y: 4, z: 4, core: 2. Of those that a mesh axis runs over, the one named last changes fastest.
Arguments:
- spectra: bfloat16 [2, 20, 32, 4096], P(None, None, None, ('col', 'row')), may hold values from -6 to 6
Outputs:
- lag_partials: float32 [32, 4096, 4096], P(None, 'row', 'col')
All inputs are finite; a program needn't handle non-finite values.
Results may differ from a plain program's by a relative error of at most 0.0029.
Values may be sent and summed in bfloat16 or wider, within the bound.
A program may use at most 256 MiB of HBM per device.

v0:
```python
import math

import jax
import jax.numpy as jnp
from jax import lax
from jax.sharding import PartitionSpec as P


def twiddle(block):
    nfreq = block.shape[2]
    nwin = block.shape[1]
    count = block.shape[3]
    scale = 1.0 / math.sqrt(2.0 * nwin * nfreq)
    lag_index = jnp.arange(nfreq, dtype=jnp.int32)[:, None]
    freq_index = jnp.arange(nfreq, dtype=jnp.int32)[None, :]
    phase = (lag_index * freq_index % nfreq).astype(jnp.float32) * (2.0 * math.pi / nfreq)
    cosine = jnp.cos(phase)[:, None, :, None]
    sine = jnp.sin(phase)[:, None, :, None]
    real_part = block[0].astype(jnp.float32)[None]
    imag_part = block[1].astype(jnp.float32)[None]
    first = scale * (real_part * cosine + imag_part * sine)
    second = scale * (imag_part * cosine - real_part * sine)
    stacked = jnp.stack([first, second], axis=1)
    stacked = jnp.transpose(stacked, (0, 4, 1, 2, 3)).reshape(nfreq, count, 2 * nwin * nfreq)
    return stacked.astype(jnp.bfloat16)


def on_device(spectra):
    nwin = spectra.shape[1]
    nfreq = spectra.shape[2]
    local_count = spectra.shape[3]
    row_count = lax.axis_size("row")
    col_count = lax.axis_size("col")
    row_size = local_count * col_count
    row_place = lax.axis_index("row")
    everything = lax.all_gather(spectra, ("row", "col"), axis=3, tiled=True)
    ordered = everything.reshape(2, nwin, nfreq, row_count, col_count, local_count)
    ordered = jnp.transpose(ordered, (0, 1, 2, 4, 3, 5)).reshape(2, nwin, nfreq, -1)
    first_rows = lax.dynamic_slice_in_dim(ordered, row_place * row_size, row_size, 3)
    twiddled = twiddle(first_rows)
    piece = lax.all_gather(spectra, "row", axis=3, tiled=True)
    right = piece.reshape(-1, piece.shape[3])
    return jnp.einsum("lik,kj->lij", twiddled, right, preferred_element_type=jnp.float32)


def solution(mesh):
    return jax.shard_map(
        on_device,
        mesh=mesh,
        in_specs=(P(None, None, None, ("col", "row")),),
        out_specs=P(None, "row", "col"),
        check_vma=False,
    )
```

profile of v0, /device:TPU:35, one launch (start us, length us, event | category | flops | bytes accessed | tf_op | source)
XLA Modules:
  0.0 491.7 jit_solution(6273250409899531770)
XLA Ops:
  6.5 0.0 all-gather.3.cloned.1.call-start
  6.5 1.9 copy.3
  8.4 0.0 all-gather.3.cloned.1.call-update
  8.4 0.0 all-gather.5.cloned.1.call-start
  8.5 0.7 all-gather.5.cloned.1.call-update
  9.2 0.1 fusion.16
  9.3 251.1 %all-gather.3.cloned.1.call-done = bf16[2,20,32,4096]{2,0,1,3:T(2,128)(2,1)} async-done(((bf16[2,20,32,32]{2,0,1,3:T(2,128)(2,1)}), bf16[2,20,32,4096]{2,0,1,3:T(2,128)(2,1)}) %all-gather.3.cloned.1.call-update) | async-done | bytes 10485776 | tf_op jit(solution)/shard_map/all_gather | solution.py:36
  260.4 113.0 %copy.4 = bf16[2,20,32,4,32,32]{5,4,3,2,1,0:T(8,128)(2,1)} copy(bf16[2,20,32,4,32,32]{2,0,1,5,3,4:T(2,128)(2,1)} %bitcast.36) | data formatting | bytes 20971520 | tf_op jit(solution)/shard_map/transpose | solution.py:38
  373.4 51.8 %reshape.70 = bf16[2,20,32,4096]{3,2,1,0:T(8,128)(2,1)} reshape(bf16[2,20,32,4,32,32]{5,4,3,2,1,0:T(8,128)(2,1)} %copy.4) | data formatting | bytes 20971520 | tf_op jit(solution)/shard_map/reshape | solution.py:38
  425.2 1.1 fusion.9
  426.3 6.1 %multiply_convert_fusion.1 = (bf16[32,1,20,32,128]{4,3,2,1,0:T(8,128)(2,1)}, bf16[32,1,20,32,128]{4,3,2,1,0:T(8,128)(2,1)}) fusion(f32[32,32]{1,0:T(8,128)S(1)} %get-tuple-element.9, f32[20,32,128]{2,1,0:T(8,128)S(1)} %get-tuple-element.6, f32[32,32]{1,0:T(8,128)S(1)} %get-tuple-element.10, f32[20,32,128]{2,1,0:T(8,128)S(1)} %get-tuple-element.5), kind=kLoop, calls=%fused_computation.7 | loop fusion | flops 26214400 | bytes 11149312 | tf_op jit(solution)/shard_map/convert.2
  432.3 0.0 all-gather.5.cloned.1.call-done
  432.3 52.5 %fusion.5 = f32[32,128,1024]{2,1,0:T(8,128)} fusion(bf16[2,20,32,1024,1]{2,0,1,3,4:T(2,128)(2,1)} %bitcast.37, bf16[32,1,20,32,128]{4,3,2,1,0:T(8,128)(2,1)} %get-tuple-element.8, bf16[32,1,20,32,128]{4,3,2,1,0:T(8,128)(2,1)} %get-tuple-element.7), kind=kOutput, calls=%fused_computation.8 | convolution fusion | flops 10742661120 | bytes 29884416 | tf_op jit(solution)/shard_map/lik,kj->lij/dot_general | solution.py:43
Async XLA Ops:
  6.5 253.9 %all-gather.3.cloned.1.call-start = ((), (), s32[]{:S(2)}) async-start(), calls=%async_computation | async-start | bytes 42270720 | tf_op jit(solution)/shard_map/all_gather | solution.py:36
  8.4 423.9 %all-gather.5.cloned.1.call-start = ((), (), s32[]{:S(2)}) async-start(), calls=%async_computation.1 | async-start | bytes 10813440 | tf_op jit(solution)/shard_map/all_gather | solution.py:41
Sparse Core Ops, SparseCore 0:
  9.1 251.2 all-gather.2
  262.0 148.0 all-gather.4
where the time goes:
time: 498 us; the launch traced here: 492 us
  waiting for transfers between devices  252 us (51%)
  local copies, waits for them, and re-layouts  167 us (34%)
  matrix products  52.5 us (11%)
  between operations  13.4 us (3%)
  other arithmetic  7.23 us (1%)
    all_gather x1, waiting for transfers between devices, on_device(): everything = lax.all_gather(spectra, ('row', 'col'), axis=3, tiled=True)  251 us
    transpose x1, local copies, waits for them, and re-layouts, on_device(): jnp.transpose(ordered, (0, 1, 2, 4, 3, 5)).reshape(2, nwin, nfreq, -1)  113 us
    dot_general x1, matrix products, on_device(): jnp.einsum('lik,kj->lij', twiddled, right, preferred_element_type=jnp.flo...  52.5 us
    reshape x1, local copies, waits for them, and re-layouts, on_device(): jnp.transpose(ordered, (0, 1, 2, 4, 3, 5)).reshape(2, nwin, nfreq, -1)  51.8 us
  transfers between devices with their start and end apart: 2, of which 1 were waited for; matrix products, arithmetic and copies ran while one was open for 35% of the time, Pallas kernels for 0%

commit v1 on v0

v1 whole, which is shorter than its diff:
```python
import functools
import math

import jax
import jax.numpy as jnp
import numpy as np
from jax import lax
from jax.experimental import pallas as pl
from jax.experimental.pallas import tpu as pltpu
from jax.sharding import PartitionSpec as P

NW, NF, NC, NR = 20, 32, 32, 32
DEPTH = 2 * NW * NF
LANE = 128
SCALE = 1.0 / math.sqrt(float(DEPTH))

PIECES = 2
PLAN = (
    (0, 0, 0), (1, 1, 0), (2, 1, 0), (3, 1, 0), (4, 1, 0), (0, 1, 0), (1, 0, 0), (2, 0, 0),
    (3, 0, 0), (4, 0, 0), (0, 1, 1), (1, 0, 16), (2, 1, 3), (3, 1, 1), (4, 1, 12), (0, 1, 3),
    (1, 1, 12), (2, 0, 4), (3, 1, 16), (4, 0, 3), (0, 0, 3), (1, 0, 12), (2, 1, 12), (3, 0, 16),
    (4, 0, 12), (0, 1, 8), (1, 1, 8), (2, 0, 3), (3, 1, 3), (4, 0, 17), (0, 1, 12), (1, 1, 17),
    (2, 1, 8), (3, 1, 19), (4, 1, 2), (0, 1, 13), (1, 0, 8), (2, 0, 7), (3, 1, 2), (4, 0, 19),
    (0, 0, 2), (1, 0, 13), (2, 0, 29), (3, 0, 7), (4, 0, 29), (0, 1, 5), (1, 0, 29), (2, 1, 23),
    (3, 0, 20), (4, 1, 19), (0, 1, 11), (1, 0, 20), (2, 0, 6), (3, 0, 19), (4, 1, 18), (0, 0, 6),
    (1, 0, 9), (3, 1, 6), (4, 0, 31), (1, 1, 24), (3, 1, 22), (4, 0, 30),
)
STEPS = ((1, 0, 0), (0, 0, 1), (0, 0, 3), (0, 1, 0), (0, 3, 0))


def split_offset(offset):
    return offset // 16, offset // 4 % 4, offset % 4


def shifted(offset, step):
    x, z, y = split_offset(offset)
    return (x + step[0]) % 2 * 16 + (z + step[1]) % 4 * 4 + (y + step[2]) % 4


CLASSES = ((0, 16, 8, 24),) + tuple((r, r + 16, 16 - r, 32 - r) for r in range(1, 8))


def lane_tables():
    cosine = np.zeros(DEPTH)
    sine = np.zeros(DEPTH)
    sign = np.zeros(DEPTH)
    for c, bins in enumerate(CLASSES):
        for part in range(2):
            for q in range(4 * NW):
                if q < 64:
                    lane = c * LANE + part * 64 + q
                else:
                    lane = 8 * LANE + c // 4 * LANE + part * 64 + c % 4 * 16 + q - 64
                which = q // NW
                phase = 2.0 * math.pi * bins[which] / NF
                cosine[lane] = SCALE * math.cos(phase)
                sine[lane] = SCALE * math.sin(phase) * (1.0 if part == 0 else -1.0)
                sign[lane] = (1.0 if which < 2 else -1.0) * (-1.0 if part == 0 else 1.0)
    table = np.zeros((8, DEPTH), np.float32)
    table[0], table[1], table[2] = cosine, sine, sign
    return table


def gather_kernel(x_ref, all_ref, first_ref, flat, ordered, own, send_sem, recv_sem, first_send, first_recv, local_sem):
    row = lax.axis_index("row")
    col = lax.axis_index("col")
    x, z, y = row // 16, row // 4 % 4, row % 4
    far, core = col // 2, col % 2
    serves = core == z // 2
    crosses = far != x

    neighbours = []
    for step in STEPS:
        neighbours.append((x + step[0]) % 2 * 16 + (z + step[1]) % 4 * 4 + (y + step[2]) % 4)
    peer = far * 2 + 1 - core
    line = z % 2 * 16 + y * 4

    barrier = pltpu.get_barrier_semaphore()
    for neighbour in neighbours:
        pl.semaphore_signal(barrier, inc=1, device_id={"row": neighbour, "col": col})
    pl.semaphore_signal(barrier, inc=1, device_id={"row": row, "col": peer})

    @pl.when(jnp.logical_and(serves, crosses))
    def _():
        for i in range(4):
            pl.semaphore_signal(barrier, inc=1, device_id={"row": line + i, "col": x * 2 + core})

    flat[...] = x_ref[...].reshape(DEPTH, NC).astype(jnp.float32)
    for c, bins in enumerate(CLASSES):
        tail = 8 * LANE + c // 4 * LANE + c % 4 * 16
        for part in range(2):
            for i, f in enumerate(bins):
                start = part * NW * NF + f
                place = c * LANE + part * 64 + i * NW
                if i < 3:
                    ordered[pl.ds(place, NW), :] = flat[pl.ds(start, NW, stride=NF), :]
                else:
                    ordered[pl.ds(place, 4), :] = flat[pl.ds(start, 4, stride=NF), :]
                    ordered[pl.ds(tail + part * 64, 16), :] = flat[pl.ds(start + 4 * NF, 16, stride=NF), :]
    for t in range(10):
        own[:, t * LANE:(t + 1) * LANE] = ordered[t * LANE:(t + 1) * LANE, :].T.astype(jnp.bfloat16)

    pl.semaphore_wait(barrier, 7)

    keep = pltpu.make_async_copy(own, all_ref.at[row], local_sem)
    keep.start()
    target_row = far * 16 + (2 * core + x) * 4 + z
    to_first = pltpu.make_async_remote_copy(
        src_ref=own, dst_ref=first_ref.at[y], send_sem=first_send.at[0], recv_sem=first_recv.at[y],
        device_id={"row": target_row, "col": (1 - far) * 2 + core},
    )

    size = NC // PIECES

    def source(offset):
        ox, oz, oy = split_offset(offset)
        return (x - ox) % 2 * 16 + (z - oz) % 4 * 4 + (y - oy) % 4

    def receive(piece, offset):
        there = all_ref.at[source(offset), pl.ds(piece * size, size)]
        sem = recv_sem.at[piece * NR + offset]
        pltpu.make_async_copy(there, there, sem).wait()

    sent = []
    arrived = {(piece, 0) for piece in range(PIECES)}
    for n, (direction, piece, offset) in enumerate(PLAN):
        if (piece, offset) not in arrived:
            receive(piece, offset)
            arrived.add((piece, offset))
        rows = pl.ds(piece * size, size)
        place = all_ref.at[source(offset), rows]
        copy = pltpu.make_async_remote_copy(
            src_ref=own.at[rows] if offset == 0 else place,
            dst_ref=place,
            send_sem=send_sem.at[n],
            recv_sem=recv_sem.at[piece * NR + shifted(offset, STEPS[direction])],
            device_id={"row": neighbours[direction], "col": col},
        )
        copy.start()
        sent.append(copy)
        if n == 9:
            to_first.start()
    for direction, piece, offset in PLAN:
        place = (piece, shifted(offset, STEPS[direction]))
        if place not in arrived:
            receive(*place)
            arrived.add(place)
    keep.wait()

    def to_peer(src):
        return pltpu.make_async_remote_copy(
            src_ref=src, dst_ref=first_ref, send_sem=first_send.at[1], recv_sem=first_recv.at[4],
            device_id={"row": row, "col": peer},
        )

    @pl.when(serves)
    def _():
        @pl.when(crosses)
        def _():
            for i in range(4):
                pltpu.make_async_copy(first_ref.at[i], first_ref.at[i], first_recv.at[i]).wait()
            copy = to_peer(first_ref)
            copy.start()
            copy.wait_send()

        @pl.when(jnp.logical_not(crosses))
        def _():
            lines = all_ref.at[pl.ds(line, 4)]
            copy = to_peer(lines)
            copy.start()
            mine = pltpu.make_async_copy(lines, first_ref, local_sem)
            mine.start()
            mine.wait()
            copy.wait_send()

    @pl.when(jnp.logical_not(serves))
    def _():
        pltpu.make_async_copy(first_ref, first_ref, first_recv.at[4]).wait()

    to_first.wait_send()
    for copy in sent:
        copy.wait_send()


def butterflies(zero, eight, real, imag):
    c1, c2, c3 = (math.cos(math.pi * k / 8) for k in (1, 2, 3))
    e = [zero] + real + [eight]
    u0, u1, u2, u3, u4 = e[0] + e[8], e[1] + e[7], e[2] + e[6], e[3] + e[5], e[4]
    d0, d1, d2, d3 = e[0] - e[8], e[1] - e[7], e[2] - e[6], e[3] - e[5]
    v0, v1 = u0 + u4, u1 + u3
    w0, w1 = u0 - u4, c2 * (u1 - u3)
    g = c2 * d2
    h0, h1 = d0 + g, d0 - g
    p, q = c1 * d1 + c3 * d3, c3 * d1 - c1 * d3
    v2 = v0 + u2
    even = [v2 + v1, h0 + p, w0 + w1, h1 + q, v0 - u2, h1 - q, w0 - w1, h0 - p, v2 - v1]
    f = [None] + imag
    s1, s2, s3 = f[1] + f[7], f[2] + f[6], f[3] + f[5]
    t1, t2, t3 = f[1] - f[7], f[2] - f[6], f[3] - f[5]
    g = c2 * s2
    a, b = c3 * s1 + c1 * s3, c1 * s1 - c3 * s3
    g0, g1 = g + f[4], g - f[4]
    k = c2 * (t1 + t3)
    odd = [None, a + g0, k + t2, b + g1, t1 - t3, b - g1, k - t2, a - g0]
    out = [even[0]] + [even[m] - odd[m] for m in range(1, 8)] + [even[8]]
    return out + [even[m] + odd[m] for m in range(7, 0, -1)]


TILE = 256
BAND = 32


def product_kernel(table_ref, first_ref, all_ref, out_ref, left, prod, outs, sems):
    lane = lax.broadcasted_iota(jnp.int32, (LANE, LANE), 1) % 64

    def variants(t):
        span = slice(t * LANE, (t + 1) * LANE)
        value = first_ref[:, span].astype(jnp.float32)
        turned = pltpu.roll(value, 64, 1)
        one = value * table_ref[0:1, span] + turned * table_ref[1:2, span]
        sign = table_ref[2:3, span]
        plain = [value * SCALE, one]
        return plain, [turned * (sign * SCALE), pltpu.roll(one, 64, 1) * sign]

    tails = [variants(8), variants(9)]
    for c in range(8):
        plain, turned = variants(c)
        tail_plain, tail_turned = tails[c // 4]
        here = lane // 16 == c % 4
        for lag in range(2):
            if c == 0:
                real = [jnp.where(lane < 40, plain[lag], 0.0), jnp.zeros_like(plain[lag])]
                imag = [jnp.where(lane < 40, 0.0, plain[lag]), jnp.where(here, tail_plain[lag], 0.0)]
            else:
                real = [plain[lag], jnp.where(here, tail_plain[lag], 0.0)]
                imag = [turned[lag], jnp.where(here, tail_turned[lag], 0.0)]
            for kind, pair in enumerate((real, imag)):
                rows = slice((kind * 2 + lag) * LANE, (kind * 2 + lag + 1) * LANE)
                left[c, rows, :LANE] = pair[0].astype(jnp.bfloat16)
                left[c, rows, LANE:] = pair[1].astype(jnp.bfloat16)

    def writes(tile, band):
        slot = lax.rem(tile, 2)
        rows = pl.ds(band * BAND, BAND)
        return pltpu.make_async_copy(
            outs.at[slot, :, rows],
            out_ref.at[:, rows, pl.ds(pl.multiple_of(tile * TILE, TILE), TILE)],
            sems.at[slot, band],
        )

    bands = LANE // BAND
    tiles = out_ref.shape[2] // TILE

    @pl.loop(0, tiles)
    def _(tile):
        slot = lax.rem(tile, 2)
        rows = pl.ds(pl.multiple_of(tile * TILE, TILE), TILE)
        for c in range(8):
            right = jnp.concatenate(
                [all_ref[rows, c * LANE:(c + 1) * LANE], all_ref[rows, (8 + c // 4) * LANE:(9 + c // 4) * LANE]], axis=1
            )
            prod[c] = lax.dot_general(left[c], right, (((1,), (1,)), ((), ())), preferred_element_type=jnp.float32)

        @pl.loop(0, bands)
        def _(band):
            @pl.when(tile >= 2)
            def _():
                writes(tile - 2, band).wait()

            @pl.loop(0, BAND // 8)
            def _(block):
                start = pl.multiple_of(band * BAND + block * 8, 8)
                for lag in range(2):
                    real = [prod[c, pl.ds(lag * LANE + start, 8), :] for c in range(8)]
                    imag = [prod[c, pl.ds((2 + lag) * LANE + start, 8), :] for c in range(8)]
                    lags = butterflies(real[0], imag[0], real[1:], imag[1:])
                    for m in range(16):
                        outs[slot, lag + 2 * m, pl.ds(start, 8), :] = lags[m]

            writes(tile, band).start()

    for tile in range(max(tiles - 2, 0), tiles):
        for band in range(bands):
            writes(tile, band).wait()


def on_device(spectra):
    gathered, first = pl.pallas_call(
        gather_kernel,
        out_shape=(
            jax.ShapeDtypeStruct((NR, NC, DEPTH), jnp.bfloat16),
            jax.ShapeDtypeStruct((4, NC, DEPTH), jnp.bfloat16),
        ),
        in_specs=[pl.BlockSpec(memory_space=pltpu.VMEM)],
        out_specs=(pl.BlockSpec(memory_space=pl.ANY), pl.BlockSpec(memory_space=pl.ANY)),
        scratch_shapes=[
            pltpu.VMEM((DEPTH, NC), jnp.float32),
            pltpu.VMEM((DEPTH, NC), jnp.float32),
            pltpu.VMEM((NC, DEPTH), jnp.bfloat16),
            pltpu.SemaphoreType.DMA((len(PLAN),)),
            pltpu.SemaphoreType.DMA((PIECES * NR,)),
            pltpu.SemaphoreType.DMA((2,)),
            pltpu.SemaphoreType.DMA((5,)),
            pltpu.SemaphoreType.DMA,
        ],
        compiler_params=pltpu.CompilerParams(
            collective_id=0, has_side_effects=True, vmem_limit_bytes=16 * 1024 * 1024
        ),
        name="gather",
    )(spectra)
    table = jnp.asarray(lane_tables())
    return pl.pallas_call(
        product_kernel,
        out_shape=jax.ShapeDtypeStruct((NF, 4 * NC, NR * NC), jnp.float32),
        in_specs=[pl.BlockSpec(memory_space=pltpu.VMEM)] * 3,
        out_specs=pl.BlockSpec(memory_space=pl.ANY),
        scratch_shapes=[
            pltpu.VMEM((8, 4 * LANE, 2 * LANE), jnp.bfloat16),
            pltpu.VMEM((8, 4 * LANE, TILE), jnp.float32),
            pltpu.VMEM((2, NF, LANE, TILE), jnp.float32),
            pltpu.SemaphoreType.DMA((2, LANE // BAND)),
        ],
        compiler_params=pltpu.CompilerParams(vmem_limit_bytes=40 * 1024 * 1024),
        name="product",
    )(table, first.reshape(4 * NC, DEPTH), gathered.reshape(NR * NC, DEPTH))


def solution(mesh):
    return jax.shard_map(
        on_device,
        mesh=mesh,
        in_specs=(P(None, None, None, ("col", "row")),),
        out_specs=P(None, "row", "col"),
        check_vma=False,
    )
```

time: 498 us -> 43.8 us (0.09)
  the two profiles are of different devices: /device:TPU:35 before, /device:TPU:3 now
where the time goes in v1:
time: 43.8 us; the launch traced here: 43.6 us
  Pallas kernels  41.9 us (96%)
  local copies, waits for them, and re-layouts  1.75 us (4%)
    pallas_call x1, Pallas kernels, on_device(): pl.pallas_call(gather_kernel, out_shape=(jax.ShapeDtypeStruct((NR, NC, DE...  33.6 us
    pallas_call x1, Pallas kernels, on_device(): pl.pallas_call(product_kernel, out_shape=jax.ShapeDtypeStruct((NF, 4 * NC...  8.31 us
    unnamed x4, local copies, waits for them, and re-layouts  1.75 us

profile of v1, /device:TPU:3, one launch (start us, length us, event | category | flops | bytes accessed | tf_op | source)
XLA Modules:
  0.0 43.6 jit_solution(4025314245879259632)
XLA Ops:
  0.0 0.0 copy-start
  0.0 1.0 %copy-done = bf16[2,20,32,32]{3,2,1,0:T(8,128)(2,1)S(1)} copy-done((bf16[2,20,32,32]{3,2,1,0:T(8,128)(2,1)S(1)}, bf16[2,20,32,32]{3,2,1,0:T(8,128)(2,1)}, u32[]{:S(2)}) %copy-start) | copy-done | bytes 81944
  1.0 33.6 %gather.1 = (bf16[32,32,1280]{2,1,0:T(8,128)(2,1)S(1)}, bf16[4,32,1280]{2,1,0:T(8,128)(2,1)S(1)}) custom-call(bf16[2,20,32,32]{3,2,1,0:T(8,128)(2,1)S(1)} %copy-done), custom_call_target="tpu_custom_call" | custom-call | tf_op jit(solution)/shard_map/gather/pallas_call | solution.py:288
  34.6 0.0 copy-start.1
  34.6 0.8 %copy-done.1 = f32[8,1280]{1,0:T(8,128)S(1)} copy-done((f32[8,1280]{1,0:T(8,128)S(1)}, f32[8,1280]{1,0:T(8,128)}, u32[]{:S(2)}) %copy-start.1) | copy-done | bytes 40984
  35.3 8.3 %product.1 = f32[32,128,1024]{2,1,0:T(8,128)} custom-call(f32[8,1280]{1,0:T(8,128)S(1)} %copy-done.1, bf16[128,1280]{1,0:T(8,128)(2,1)S(1)} %bitcast.3, bf16[1024,1280]{1,0:T(8,128)(2,1)S(1)} %bitcast.2), custom_call_target="tpu_custom_call" | custom-call | tf_op jit(solution)/shard_map/product/pallas_call | solution.py:312
Async XLA Ops:
  0.0 1.0 %copy-start = (bf16[2,20,32,32]{3,2,1,0:T(8,128)(2,1)S(1)}, bf16[2,20,32,32]{3,2,1,0:T(8,128)(2,1)}, u32[]{:S(2)}) copy-start(bf16[2,20,32,32]{3,2,1,0:T(8,128)(2,1)} %x_ref.1) | copy-start | bytes 245764
  34.6 0.8 %copy-start.1 = (f32[8,1280]{1,0:T(8,128)S(1)}, f32[8,1280]{1,0:T(8,128)}, u32[]{:S(2)}) copy-start(f32[8,1280]{1,0:T(8,128)} %constant.2.clone.table_ref) | copy-start | bytes 122884

commit v2 on v0

v2 whole, which is shorter than its diff:
```python
import functools
import math

import jax
import jax.numpy as jnp
from jax import lax
from jax.experimental import pallas as pl
from jax.experimental.pallas import tpu as pltpu
from jax.sharding import PartitionSpec as P

NW, NF, NC, NR = 20, 32, 32, 32
DEPTH = 2 * NW * NF
LANE = 128
SCALE = 1.0 / math.sqrt(float(DEPTH))

PLAN_0 = (
    (2, 0, 0), (11, 1, 0), (3, 0, 0), (3, 1, 0), (4, 0, 0), (6, 0, 0), (6, 1, 0), (1, 1, 0),
    (2, 1, 0), (1, 0, 0), (4, 1, 0), (0, 1, 0), (0, 0, 0), (0, 0, 3), (2, 0, 3), (4, 0, 3),
    (3, 1, 3), (0, 1, 3), (4, 1, 28), (2, 1, 28), (1, 1, 28), (3, 1, 16), (0, 0, 5), (3, 0, 5),
    (4, 0, 12), (1, 1, 12), (2, 1, 12), (1, 1, 5), (10, 0, 5), (4, 0, 16), (2, 0, 4), (1, 1, 1),
    (10, 0, 3), (0, 0, 1), (4, 1, 12), (2, 0, 19), (4, 0, 19), (0, 1, 1), (4, 0, 15), (7, 1, 19),
    (3, 1, 7), (1, 1, 29), (4, 1, 29), (2, 1, 24), (-1, 0, 2), (0, 1, 7), (2, 1, 19), (1, 1, 13),
    (0, 0, 8), (1, 1, 20), (3, 0, 9), (4, 1, 13), (-1, 1, 4), (3, 1, 6), (2, 0, 15), (0, 0, 4),
    (1, 0, 25), (-1, 1, 15), (2, 0, 7), (4, 0, 18), (1, 0, 21), (-1, 1, 2), (-1, 1, 31), (-1, 0, 23),
    (3, 0, 25), (-1, 0, 17), (-1, 1, 8), (-1, 0, 28), (4, 0, 31), (2, 0, 11), (3, 1, 22), (-1, 1, 17),
    (-1, 1, 27), (-1, 1, 14), (-1, 1, 23), (-1, 1, 18), (-1, 1, 25), (-1, 1, 11), (-1, 1, 30), (-1, 0, 13),
    (-1, 1, 21), (-1, 0, 24), (-1, 0, 14), (-1, 1, 9), (-1, 0, 20), (-1, 0, 30), (-1, 0, 6), (-1, 1, 10),
    (-1, 0, 26), (-1, 0, 22), (-1, 0, 29), (-1, 0, 27), (-1, 0, 10), (-1, 1, 26),
)
PLAN_1 = (
    (3, 0, 0), (0, 1, 0), (5, 1, 0), (4, 0, 0), (1, 0, 0), (2, 0, 0), (4, 1, 0), (0, 0, 0),
    (2, 1, 0), (3, 1, 0), (1, 1, 0), (3, 0, 4), (0, 0, 4), (8, 1, 16), (1, 0, 4), (0, 0, 12),
    (4, 1, 16), (2, 0, 4), (1, 1, 16), (3, 1, 16), (0, 0, 1), (3, 1, 2), (8, 0, 12), (8, 0, 3),
    (1, 1, 4), (0, 1, 2), (3, 1, 3), (3, 1, 4), (-1, 0, 16), (1, 0, 8), (9, 0, 8), (1, 0, 5),
    (0, 0, 5), (4, 0, 28), (3, 1, 20), (1, 0, 28), (2, 0, 28), (0, 0, 7), (4, 1, 31), (1, 0, 17),
    (3, 1, 6), (4, 0, 3), (1, 1, 12), (4, 1, 2), (2, 1, 31), (0, 1, 5), (4, 1, 17), (3, 1, 7),
    (2, 0, 11), (3, 1, 18), (-1, 1, 28), (0, 0, 9), (4, 0, 1), (0, 1, 3), (-1, 0, 20), (2, 0, 27),
    (0, 1, 7), (1, 1, 24), (3, 0, 14), (-1, 0, 24), (2, 0, 31), (1, 1, 8), (0, 0, 6), (4, 0, 23),
    (-1, 1, 10), (-1, 0, 29), (2, 1, 27), (-1, 1, 1), (3, 1, 11), (-1, 1, 30), (-1, 1, 21), (-1, 0, 15),
    (-1, 0, 21), (-1, 0, 25), (-1, 1, 13), (-1, 0, 10), (-1, 1, 14), (-1, 0, 26), (-1, 1, 22), (-1, 1, 29),
    (-1, 0, 2), (-1, 0, 18), (-1, 1, 25), (-1, 1, 19), (-1, 0, 30), (-1, 1, 9), (-1, 1, 23), (-1, 0, 13),
    (-1, 1, 26), (-1, 0, 19), (-1, 1, 15), (-1, 0, 22),
)
PLANS = (PLAN_0, PLAN_1)
PIECES = 2
STEPS = (
    (1, 0, 0), (0, 0, 1), (0, 0, 3), (0, 1, 0), (0, 3, 0), (0, 0, 2), (0, 1, 1), (0, 1, 3),
    (0, 3, 3), (1, 0, 3), (1, 1, 0), (1, 3, 0),
)


def steps_of(plan):
    return sorted({STEPS[entry[0]] for entry in plan if entry[0] >= 0})


def split_offset(offset):
    return offset // 16, offset // 4 % 4, offset % 4


def shifted(offset, step):
    x, z, y = split_offset(offset)
    return (x + step[0]) % 2 * 16 + (z + step[1]) % 4 * 4 + (y + step[2]) % 4


CLASSES = ((0, 16, 8, 24),) + tuple((r, r + 16, 16 - r, 32 - r) for r in range(1, 8))


def gather_kernel(x_ref, all_ref, first_ref, flat, ordered, own, send_sem, recv_sem, first_send, first_recv, local_sem):
    row = lax.axis_index("row")
    col = lax.axis_index("col")
    x, z, y = row // 16, row // 4 % 4, row % 4
    far, core = col // 2, col % 2
    peer = {"row": row, "col": far * 2 + 1 - core}
    other = {"row": (1 - x) * 16 + row % 16, "col": (1 - far) * 2 + core}
    serves = core == z // 2
    passes = jnp.logical_and(serves, far != x)
    keeps = jnp.logical_and(serves, far == x)
    line = z % 2 * 4 + y
    size = NC // PIECES

    def there(step):
        return (x + step[0]) % 2 * 16 + (z + step[1]) % 4 * 4 + (y + step[2]) % 4

    def source(offset):
        ox, oz, oy = split_offset(offset)
        return (x - ox) % 2 * 16 + (z - oz) % 4 * 4 + (y - oy) % 4

    barrier = pltpu.get_barrier_semaphore()
    for which, plan in enumerate(PLANS):

        @pl.when(core == which)
        def _():
            for step in steps_of(plan):
                behind = ((-step[0]) % 2, (-step[1]) % 4, (-step[2]) % 4)
                pl.semaphore_signal(barrier, inc=1, device_id={"row": there(behind), "col": col})

    pl.semaphore_signal(barrier, inc=1, device_id=peer)
    pl.semaphore_signal(barrier, inc=1, device_id=other)

    flat[...] = x_ref[...].reshape(DEPTH, NC).astype(jnp.float32)
    for c, bins in enumerate(CLASSES):
        tail = 8 * LANE + c // 4 * LANE + c % 4 * 16
        for part in range(2):
            for i, f in enumerate(bins):
                start = part * NW * NF + f
                place = c * LANE + part * 64 + i * NW
                if i < 3:
                    ordered[pl.ds(place, NW), :] = flat[pl.ds(start, NW, stride=NF), :]
                else:
                    ordered[pl.ds(place, 4), :] = flat[pl.ds(start, 4, stride=NF), :]
                    ordered[pl.ds(tail + part * 64, 16), :] = flat[pl.ds(start + 4 * NF, 16, stride=NF), :]
    for t in range(10):
        own[:, t * LANE:(t + 1) * LANE] = ordered[t * LANE:(t + 1) * LANE, :].T.astype(jnp.bfloat16)

    keep = pltpu.make_async_copy(own, all_ref.at[row], local_sem)
    keep.start()

    def first_copy(src, index, slot, piece, device):
        return pltpu.make_async_remote_copy(
            src_ref=src, dst_ref=first_ref.at[slot, pl.ds(piece * size, size)], send_sem=first_send.at[index],
            recv_sem=first_recv.at[index], device_id=device,
        )

    def part(index, sem):
        place = first_ref.at[index // PIECES, pl.ds(index % PIECES * size, size)]
        return pltpu.make_async_copy(place, place, sem)

    def serve(piece, offset):
        origin = source(offset)
        rows = pl.ds(piece * size, size)
        src = own.at[rows] if offset == 0 else all_ref.at[origin, rows]
        slot = origin % 4
        index = slot * PIECES + piece
        wanted = origin // 4 == line

        @pl.when(jnp.logical_and(wanted, passes))
        def _():
            first_copy(src, index, slot, piece, other).start()

        @pl.when(jnp.logical_and(wanted, keeps))
        def _():
            first_copy(src, index, slot, piece, peer).start()
            pltpu.make_async_copy(src, first_ref.at[slot, rows], first_recv.at[index]).start()

    def move(plan):
        pl.semaphore_wait(barrier, len(steps_of(plan)) + 2)
        sent = []
        seen = set()
        for n, (step, piece, offset) in enumerate(plan):
            rows = pl.ds(piece * size, size)
            place = all_ref.at[source(offset), rows]
            fresh = (piece, offset) not in seen
            seen.add((piece, offset))
            if fresh and offset:
                pltpu.make_async_copy(place, place, recv_sem.at[piece * NR + offset]).wait()
            if step >= 0:
                copy = pltpu.make_async_remote_copy(
                    src_ref=own.at[rows] if offset == 0 else place,
                    dst_ref=place,
                    send_sem=send_sem.at[len(sent)],
                    recv_sem=recv_sem.at[piece * NR + shifted(offset, STEPS[step])],
                    device_id={"row": there(STEPS[step]), "col": col},
                )
                copy.start()
                sent.append(copy)
            if fresh:
                serve(piece, offset)
        assert len(seen) == PIECES * NR and len(sent) == PIECES * (NR - 1)
        return sent

    for which, plan in enumerate(PLANS):

        @pl.when(core == which)
        def _():
            sent = move(plan)
            for index in range(4 * PIECES):
                part(index, first_recv.at[index]).wait()

                @pl.when(passes)
                def _():
                    pltpu.make_async_remote_copy(
                        src_ref=first_ref.at[index // PIECES, pl.ds(index % PIECES * size, size)],
                        dst_ref=first_ref.at[index // PIECES, pl.ds(index % PIECES * size, size)],
                        send_sem=first_send.at[4 * PIECES + index], recv_sem=first_recv.at[index], device_id=peer,
                    ).start()

            for copy in sent:
                copy.wait_send()

    keep.wait()

    @pl.when(serves)
    def _():
        for index in range(4 * PIECES):
            part(index, first_send.at[index]).wait()

    @pl.when(passes)
    def _():
        for index in range(4 * PIECES):
            part(index, first_send.at[4 * PIECES + index]).wait()


def butterflies(zero, eight, real, imag):
    c1, c2, c3 = (math.cos(math.pi * k / 8) for k in (1, 2, 3))
    e = [zero] + real + [eight]
    u0, u1, u2, u3, u4 = e[0] + e[8], e[1] + e[7], e[2] + e[6], e[3] + e[5], e[4]
    d0, d1, d2, d3 = e[0] - e[8], e[1] - e[7], e[2] - e[6], e[3] - e[5]
    v0, v1 = u0 + u4, u1 + u3
    w0, w1 = u0 - u4, c2 * (u1 - u3)
    g = c2 * d2
    h0, h1 = d0 + g, d0 - g
    p, q = c1 * d1 + c3 * d3, c3 * d1 - c1 * d3
    v2 = v0 + u2
    even = [v2 + v1, h0 + p, w0 + w1, h1 + q, v0 - u2, h1 - q, w0 - w1, h0 - p, v2 - v1]
    f = [None] + imag
    s1, s2, s3 = f[1] + f[7], f[2] + f[6], f[3] + f[5]
    t1, t2, t3 = f[1] - f[7], f[2] - f[6], f[3] - f[5]
    g = c2 * s2
    a, b = c3 * s1 + c1 * s3, c1 * s1 - c3 * s3
    g0, g1 = g + f[4], g - f[4]
    k = c2 * (t1 + t3)
    odd = [None, a + g0, k + t2, b + g1, t1 - t3, b - g1, k - t2, a - g0]
    out = [even[0]] + [even[m] - odd[m] for m in range(1, 8)] + [even[8]]
    return out + [even[m] + odd[m] for m in range(7, 0, -1)]


TILE = 256
BAND = 64
WIDE = 256


def product_kernel(first_ref, all_ref, out_ref, left, prod_0, prod_1, outs, sems):
    prods = (prod_0, prod_1)
    lane = lax.broadcasted_iota(jnp.int32, (LANE, LANE), 1)
    place = lane % 64
    turn = jnp.where(lane < 64, 1.0, -1.0)

    def choose(values, edges):
        out = jnp.full((LANE, LANE), values[-1], jnp.float32)
        for value, edge in zip(values[-2::-1], edges[::-1]):
            out = jnp.where(place < edge, value, out)
        return out

    def phases(t):
        if t < 8:
            bins, edges, signs = CLASSES[t], (20, 40, 60), (1.0, 1.0, -1.0, -1.0)
        else:
            bins, edges, signs = tuple(CLASSES[4 * (t - 8) + i][3] for i in range(4)), (16, 32, 48), (-1.0,) * 4
        angle = [2.0 * math.pi * f / NF for f in bins]
        cosine = choose([SCALE * math.cos(v) for v in angle], edges)
        sine = choose([SCALE * math.sin(v) for v in angle], edges) * turn
        return cosine, sine, choose(signs, edges) * -turn

    def variants(t):
        value = first_ref[:, t * LANE:(t + 1) * LANE].astype(jnp.float32)
        cosine, sine, sign = phases(t)
        turned = pltpu.roll(value, 64, 1)
        one = value * cosine + turned * sine
        return [value * SCALE, one], [turned * (sign * SCALE), pltpu.roll(one, 64, 1) * sign]

    def prepare(c, tail):
        plain, turned = variants(c)
        tail_plain, tail_turned = tail
        here = place // 16 == c % 4
        for lag in range(2):
            if c == 0:
                real = [jnp.where(place < 40, plain[lag], 0.0), jnp.zeros_like(plain[lag])]
                imag = [jnp.where(place < 40, 0.0, plain[lag]), jnp.where(here, tail_plain[lag], 0.0)]
            else:
                real = [plain[lag], jnp.where(here, tail_plain[lag], 0.0)]
                imag = [turned[lag], jnp.where(here, tail_turned[lag], 0.0)]
            for kind, pair in enumerate((real, imag)):
                rows = slice((kind * 2 + lag) * LANE, (kind * 2 + lag + 1) * LANE)
                left[c, rows, :LANE] = pair[0].astype(jnp.bfloat16)
                left[c, rows, LANE:] = pair[1].astype(jnp.bfloat16)

    def multiply(prod, tile, c):
        rows = pl.ds(tile * TILE, TILE)
        if isinstance(c, int):
            main, tail = pl.ds(c * LANE, LANE), pl.ds((8 + c // 4) * LANE, LANE)
        else:
            main = pl.ds(pl.multiple_of(c * LANE, LANE), LANE)
            tail = pl.ds(pl.multiple_of((8 + c // 4) * LANE, LANE), LANE)
        right = jnp.concatenate([all_ref[rows, main], all_ref[rows, tail]], axis=1)
        prod[c] = lax.dot_general(left[c], right, (((1,), (1,)), ((), ())), preferred_element_type=jnp.float32)

    def combine(prod, slot, band):
        for block in range(BAND // 8):
            start = pl.multiple_of(band * BAND + block * 8, 8)
            for lag in range(2):
                for half in range(TILE // WIDE):
                    span = slice(half * WIDE, (half + 1) * WIDE)
                    real = [prod[c, pl.ds(lag * LANE + start, 8), span] for c in range(8)]
                    imag = [prod[c, pl.ds((2 + lag) * LANE + start, 8), span] for c in range(8)]
                    lags = butterflies(real[0], imag[0], real[1:], imag[1:])
                    for m in range(16):
                        outs[slot, lag + 2 * m, pl.ds(start, 8), span] = lags[m]

    def writes(tile, band):
        rows = pl.ds(band * BAND, BAND)
        return pltpu.make_async_copy(
            outs.at[tile % 2, :, rows], out_ref.at[:, rows, pl.ds(tile * TILE, TILE)], sems.at[tile % 2, band]
        )

    bands = LANE // BAND
    tiles = out_ref.shape[2] // TILE
    tails = [variants(8), variants(9)]
    for c in range(8):
        prepare(c, tails[c // 4])
        multiply(prods[0], 0, c)
    for tile in range(tiles):

        @pl.loop(0, bands)
        def _(band):
            if tile >= 2:
                writes(tile - 2, band).wait()
            if tile + 1 < tiles:
                for i in range(8 // bands):
                    multiply(prods[(tile + 1) % 2], tile + 1, band * (8 // bands) + i)
            combine(prods[tile % 2], tile % 2, band)
            writes(tile, band).start()

    for tile in range(max(tiles - 2, 0), tiles):
        for band in range(bands):
            writes(tile, band).wait()


def product_call(first, gathered):
    return pl.pallas_call(
        product_kernel,
        out_shape=jax.ShapeDtypeStruct((NF, 4 * NC, NR * NC), jnp.float32),
        in_specs=[pl.BlockSpec(memory_space=pltpu.VMEM)] * 2,
        out_specs=pl.BlockSpec(memory_space=pl.ANY),
        scratch_shapes=[
            pltpu.VMEM((8, 4 * LANE, 2 * LANE), jnp.bfloat16),
            pltpu.VMEM((8, 4 * LANE, TILE), jnp.float32),
            pltpu.VMEM((8, 4 * LANE, TILE), jnp.float32),
            pltpu.VMEM((2, NF, LANE, TILE), jnp.float32),
            pltpu.SemaphoreType.DMA((2, LANE // BAND)),
        ],
        compiler_params=pltpu.CompilerParams(vmem_limit_bytes=40 * 1024 * 1024),
        name="product",
    )(first, gathered)


def on_device(spectra):
    gathered, first = pl.pallas_call(
        gather_kernel,
        out_shape=(
            jax.ShapeDtypeStruct((NR, NC, DEPTH), jnp.bfloat16),
            jax.ShapeDtypeStruct((4, NC, DEPTH), jnp.bfloat16),
        ),
        in_specs=[pl.BlockSpec(memory_space=pltpu.VMEM)],
        out_specs=(pl.BlockSpec(memory_space=pl.ANY), pl.BlockSpec(memory_space=pl.ANY)),
        scratch_shapes=[
            pltpu.VMEM((DEPTH, NC), jnp.float32),
            pltpu.VMEM((DEPTH, NC), jnp.float32),
            pltpu.VMEM((NC, DEPTH), jnp.bfloat16),
            pltpu.SemaphoreType.DMA((PIECES * (NR - 1),)),
            pltpu.SemaphoreType.DMA((PIECES * NR,)),
            pltpu.SemaphoreType.DMA((8 * PIECES,)),
            pltpu.SemaphoreType.DMA((4 * PIECES,)),
            pltpu.SemaphoreType.DMA,
        ],
        compiler_params=pltpu.CompilerParams(
            collective_id=0, has_side_effects=True, vmem_limit_bytes=16 * 1024 * 1024
        ),
        name="gather",
    )(spectra)
    return product_call(first.reshape(4 * NC, DEPTH), gathered.reshape(NR * NC, DEPTH))


def solution(mesh):
    return jax.shard_map(
        on_device,
        mesh=mesh,
        in_specs=(P(None, None, None, ("col", "row")),),
        out_specs=P(None, "row", "col"),
        check_vma=False,
    )
```

time: 498 us -> 35.6 us (0.07); the launches traced: 492 us -> 35.1 us
  waiting for transfers between devices: 252 us -> 0 us
  local copies, waits for them, and re-layouts: 167 us -> 0.97 us
  matrix products: 52.5 us -> 0 us
  Pallas kernels: 0 us -> 34.1 us
  between operations: 13.4 us -> 0.01 us
  other arithmetic: 7.23 us -> 0 us
    all_gather x2 -> x0, waiting for transfers between devices: 251 us -> none  [the longest x1 251 us: on_device(): everything = lax.all_gather(spectra, ('row', 'col'), axis=3, tiled=True)]
    transpose x1 -> x0, local copies, waits for them, and re-layouts: 113 us -> none  [on_device(): jnp.transpose(ordered, (0, 1, 2, 4, 3, 5)).reshape(2, nwin, nfreq, -1)]
    dot_general x1 -> x0, matrix products: 52.5 us -> none  [on_device(): jnp.einsum('lik,kj->lij', twiddled, right, preferred_element_type=jnp.flo...]
    reshape x1 -> x0, local copies, waits for them, and re-layouts: 51.8 us -> none  [on_device(): jnp.transpose(ordered, (0, 1, 2, 4, 3, 5)).reshape(2, nwin, nfreq, -1)]
    pallas_call x0 -> x2, Pallas kernels: none -> 34.1 us  [the longest x1 26.4 us: on_device(): pl.pallas_call(gather_kernel, out_shape=(jax.ShapeDtypeStruct((NR, NC, DE...]
    another operation x1 -> x0, other arithmetic: 6.08 us -> none
  transfers between devices with their start and end apart: 2 -> 0, of which waited for: 1 -> 0; matrix products, arithmetic and copies ran while one was open for 35% -> 0% of each run, Pallas kernels for 0% -> 0%
where the time goes in v2:
time: 35.6 us; the launch traced here: 35.1 us
  Pallas kernels  34.1 us (96%)
  local copies, waits for them, and re-layouts  0.97 us (3%)
    pallas_call x1, Pallas kernels, on_device(): pl.pallas_call(gather_kernel, out_shape=(jax.ShapeDtypeStruct((NR, NC, DE...  26.4 us
    pallas_call x1, Pallas kernels, product_call(): pl.pallas_call(product_kernel, out_shape=jax.ShapeDtypeStruct((NF, 4 * NC...  7.7 us
    unnamed x2, local copies, waits for them, and re-layouts  0.97 us

profile of v2, /device:TPU:35, one launch (start us, length us, event | category | flops | bytes accessed | tf_op | source)
XLA Modules:
  0.0 35.1 jit_solution(17845206936364790207)
XLA Ops:
  0.0 0.0 copy-start
  0.0 1.0 %copy-done = bf16[2,20,32,32]{3,2,1,0:T(8,128)(2,1)S(1)} copy-done((bf16[2,20,32,32]{3,2,1,0:T(8,128)(2,1)S(1)}, bf16[2,20,32,32]{3,2,1,0:T(8,128)(2,1)}, u32[]{:S(2)}) %copy-start) | copy-done | bytes 81944
  1.0 26.4 %gather.1 = (bf16[32,32,1280]{2,1,0:T(8,128)(2,1)S(1)}, bf16[4,32,1280]{2,1,0:T(8,128)(2,1)S(1)}) custom-call(bf16[2,20,32,32]{3,2,1,0:T(8,128)(2,1)S(1)} %copy-done), custom_call_target="tpu_custom_call" | custom-call | tf_op jit(solution)/shard_map/gather/pallas_call | solution.py:347
  27.4 7.7 %product.1 = f32[32,128,1024]{2,1,0:T(8,128)} custom-call(bf16[128,1280]{1,0:T(8,128)(2,1)S(1)} %bitcast.3, bf16[1024,1280]{1,0:T(8,128)(2,1)S(1)} %bitcast.2), custom_call_target="tpu_custom_call" | custom-call | tf_op jit(solution)/shard_map/product/pallas_call | solution.py:329
Async XLA Ops:
  0.0 1.0 %copy-start = (bf16[2,20,32,32]{3,2,1,0:T(8,128)(2,1)S(1)}, bf16[2,20,32,32]{3,2,1,0:T(8,128)(2,1)}, u32[]{:S(2)}) copy-start(bf16[2,20,32,32]{3,2,1,0:T(8,128)(2,1)} %x_ref.1) | copy-start | bytes 245764

commit v3 on v2

--- a/solution.py
+++ b/solution.py
@@ -14,39 +14,40 @@
 SCALE = 1.0 / math.sqrt(float(DEPTH))
 
 PLAN_0 = (
-    (2, 0, 0), (11, 1, 0), (3, 0, 0), (3, 1, 0), (4, 0, 0), (6, 0, 0), (6, 1, 0), (1, 1, 0),
-    (2, 1, 0), (1, 0, 0), (4, 1, 0), (0, 1, 0), (0, 0, 0), (0, 0, 3), (2, 0, 3), (4, 0, 3),
-    (3, 1, 3), (0, 1, 3), (4, 1, 28), (2, 1, 28), (1, 1, 28), (3, 1, 16), (0, 0, 5), (3, 0, 5),
-    (4, 0, 12), (1, 1, 12), (2, 1, 12), (1, 1, 5), (10, 0, 5), (4, 0, 16), (2, 0, 4), (1, 1, 1),
-    (10, 0, 3), (0, 0, 1), (4, 1, 12), (2, 0, 19), (4, 0, 19), (0, 1, 1), (4, 0, 15), (7, 1, 19),
-    (3, 1, 7), (1, 1, 29), (4, 1, 29), (2, 1, 24), (-1, 0, 2), (0, 1, 7), (2, 1, 19), (1, 1, 13),
-    (0, 0, 8), (1, 1, 20), (3, 0, 9), (4, 1, 13), (-1, 1, 4), (3, 1, 6), (2, 0, 15), (0, 0, 4),
-    (1, 0, 25), (-1, 1, 15), (2, 0, 7), (4, 0, 18), (1, 0, 21), (-1, 1, 2), (-1, 1, 31), (-1, 0, 23),
-    (3, 0, 25), (-1, 0, 17), (-1, 1, 8), (-1, 0, 28), (4, 0, 31), (2, 0, 11), (3, 1, 22), (-1, 1, 17),
-    (-1, 1, 27), (-1, 1, 14), (-1, 1, 23), (-1, 1, 18), (-1, 1, 25), (-1, 1, 11), (-1, 1, 30), (-1, 0, 13),
-    (-1, 1, 21), (-1, 0, 24), (-1, 0, 14), (-1, 1, 9), (-1, 0, 20), (-1, 0, 30), (-1, 0, 6), (-1, 1, 10),
-    (-1, 0, 26), (-1, 0, 22), (-1, 0, 29), (-1, 0, 27), (-1, 0, 10), (-1, 1, 26),
+    (1, 1, 0), (3, 1, 0), (4, 1, 0), (0, 0, 0), (2, 1, 0), (2, 0, 0), (0, 1, 0), (6, 0, 0),
+    (1, 0, 0), (3, 0, 0), (4, 0, 0), (7, 1, 1), (1, 1, 1), (0, 1, 4), (3, 1, 4), (1, 1, 12),
+    (2, 1, 12), (0, 1, 3), (1, 0, 16), (4, 0, 1), (3, 0, 5), (2, 0, 4), (0, 0, 5), (4, 0, 12),
+    (1, 0, 5), (3, 0, 16), (2, 0, 12), (0, 1, 1), (4, 0, 16), (2, 0, 3), (1, 1, 4), (2, 0, 16),
+    (2, 1, 4), (0, 1, 12), (4, 1, 2), (3, 1, 2), (1, 1, 9), (0, 1, 9), (-1, 1, 8), (4, 1, 15),
+    (3, 1, 20), (1, 0, 13), (2, 1, 19), (1, 0, 9), (3, 0, 7), (0, 0, 8), (-1, 0, 6), (-1, 1, 13),
+    (1, 0, 21), (0, 0, 15), (2, 1, 20), (-1, 1, 5), (4, 1, 19), (-1, 0, 2), (6, 1, 17), (0, 1, 14),
+    (0, 1, 10), (4, 1, 17), (2, 1, 24), (-1, 1, 11), (-1, 1, 7), (1, 1, 20), (0, 0, 14), (-1, 0, 11),
+    (-1, 1, 6), (3, 0, 21), (4, 0, 17), (-1, 0, 10), (2, 0, 20), (1, 0, 17), (3, 0, 22), (2, 0, 24),
+    (-1, 1, 22), (-1, 1, 25), (-1, 1, 23), (-1, 1, 29), (-1, 0, 31), (-1, 0, 19), (-1, 1, 27), (-1, 1, 28),
+    (-1, 0, 28), (-1, 1, 26), (-1, 1, 30), (-1, 1, 31), (-1, 0, 25), (-1, 1, 16), (-1, 1, 21), (-1, 1, 18),
+    (-1, 0, 23), (-1, 0, 29), (-1, 0, 18), (-1, 0, 30), (-1, 0, 26), (-1, 0, 27),
 )
 PLAN_1 = (
-    (3, 0, 0), (0, 1, 0), (5, 1, 0), (4, 0, 0), (1, 0, 0), (2, 0, 0), (4, 1, 0), (0, 0, 0),
-    (2, 1, 0), (3, 1, 0), (1, 1, 0), (3, 0, 4), (0, 0, 4), (8, 1, 16), (1, 0, 4), (0, 0, 12),
-    (4, 1, 16), (2, 0, 4), (1, 1, 16), (3, 1, 16), (0, 0, 1), (3, 1, 2), (8, 0, 12), (8, 0, 3),
-    (1, 1, 4), (0, 1, 2), (3, 1, 3), (3, 1, 4), (-1, 0, 16), (1, 0, 8), (9, 0, 8), (1, 0, 5),
-    (0, 0, 5), (4, 0, 28), (3, 1, 20), (1, 0, 28), (2, 0, 28), (0, 0, 7), (4, 1, 31), (1, 0, 17),
-    (3, 1, 6), (4, 0, 3), (1, 1, 12), (4, 1, 2), (2, 1, 31), (0, 1, 5), (4, 1, 17), (3, 1, 7),
-    (2, 0, 11), (3, 1, 18), (-1, 1, 28), (0, 0, 9), (4, 0, 1), (0, 1, 3), (-1, 0, 20), (2, 0, 27),
-    (0, 1, 7), (1, 1, 24), (3, 0, 14), (-1, 0, 24), (2, 0, 31), (1, 1, 8), (0, 0, 6), (4, 0, 23),
-    (-1, 1, 10), (-1, 0, 29), (2, 1, 27), (-1, 1, 1), (3, 1, 11), (-1, 1, 30), (-1, 1, 21), (-1, 0, 15),
-    (-1, 0, 21), (-1, 0, 25), (-1, 1, 13), (-1, 0, 10), (-1, 1, 14), (-1, 0, 26), (-1, 1, 22), (-1, 1, 29),
-    (-1, 0, 2), (-1, 0, 18), (-1, 1, 25), (-1, 1, 19), (-1, 0, 30), (-1, 1, 9), (-1, 1, 23), (-1, 0, 13),
-    (-1, 1, 26), (-1, 0, 19), (-1, 1, 15), (-1, 0, 22),
+    (4, 1, 0), (3, 1, 0), (0, 0, 0), (5, 1, 0), (5, 0, 0), (1, 0, 0), (0, 1, 0), (3, 0, 0),
+    (4, 0, 0), (3, 1, 4), (2, 1, 4), (0, 1, 12), (8, 1, 12), (2, 1, 12), (3, 0, 16), (3, 0, 4),
+    (0, 1, 4), (1, 0, 12), (4, 0, 16), (2, 0, 4), (0, 1, 2), (4, 1, 2), (1, 1, 16), (2, 1, 2),
+    (1, 1, 12), (3, 0, 2), (0, 0, 2), (3, 0, 1), (4, 0, 2), (2, 1, 7), (0, 1, 7), (-1, 1, 8),
+    (3, 1, 7), (8, 1, 28), (3, 0, 20), (0, 1, 15), (1, 1, 9), (2, 0, 8), (4, 0, 13), (2, 1, 16),
+    (2, 1, 0), (2, 0, 20), (1, 1, 28), (0, 0, 13), (1, 0, 20), (3, 0, 6), (4, 1, 9), (1, 1, 20),
+    (0, 1, 14), (4, 0, 7), (3, 0, 18), (4, 1, 28), (1, 0, 18), (-1, 1, 11), (4, 0, 18), (0, 1, 6),
+    (3, 0, 11), (-1, 1, 10), (2, 0, 18), (1, 0, 24), (-1, 0, 5), (-1, 0, 9), (2, 0, 24), (3, 1, 23),
+    (0, 0, 10), (-1, 1, 5), (-1, 1, 1), (-1, 1, 13), (1, 1, 25), (2, 0, 28), (-1, 1, 3), (-1, 1, 18),
+    (-1, 0, 14), (-1, 0, 3), (-1, 1, 31), (-1, 1, 30), (-1, 0, 22), (-1, 0, 15), (-1, 0, 21), (-1, 1, 29),
+    (-1, 1, 24), (-1, 0, 23), (-1, 0, 19), (-1, 0, 29), (-1, 1, 21), (-1, 0, 17), (-1, 1, 22), (-1, 0, 25),
+    (-1, 1, 19), (-1, 0, 30), (-1, 0, 27), (-1, 1, 27), (-1, 1, 17), (-1, 0, 26), (-1, 1, 26), (-1, 0, 31),
 )
 PLANS = (PLAN_0, PLAN_1)
 PIECES = 2
 STEPS = (
-    (1, 0, 0), (0, 0, 1), (0, 0, 3), (0, 1, 0), (0, 3, 0), (0, 0, 2), (0, 1, 1), (0, 1, 3),
-    (0, 3, 3), (1, 0, 3), (1, 1, 0), (1, 3, 0),
+    (1, 0, 0), (0, 0, 1), (0, 0, 3), (0, 1, 0), (0, 3, 0), (0, 0, 2), (0, 1, 1), (0, 2, 0),
+    (0, 3, 1),
 )
+PASS_BEFORE = 8
 
 
 def steps_of(plan):
@@ -65,25 +66,42 @@
 CLASSES = ((0, 16, 8, 24),) + tuple((r, r + 16, 16 - r, 32 - r) for r in range(1, 8))
 
 
-def gather_kernel(x_ref, all_ref, first_ref, flat, ordered, own, send_sem, recv_sem, first_send, first_recv, local_sem):
+def gather_kernel(x_ref, all_ref, first_ref, raw, flat, ordered, own, send_sem, recv_sem, first_send, first_recv, local_sem):
     row = lax.axis_index("row")
     col = lax.axis_index("col")
     x, z, y = row // 16, row // 4 % 4, row % 4
     far, core = col // 2, col % 2
     peer = {"row": row, "col": far * 2 + 1 - core}
-    other = {"row": (1 - x) * 16 + row % 16, "col": (1 - far) * 2 + core}
-    serves = core == z // 2
-    passes = jnp.logical_and(serves, far != x)
+    target_row = far * 16 + z * 4 + y
+    target = {"row": target_row, "col": (1 - far) * 2 + core}
+    second = {"row": target_row, "col": far * 2 + core}
+    server = {"row": z % 2 * 16 + z * 4 + y, "col": x * 2 + core}
+    speaks = core == z // 2
+    serves = jnp.logical_and(speaks, x == z % 2)
     keeps = jnp.logical_and(serves, far == x)
-    line = z % 2 * 4 + y
+    both = jnp.logical_and(serves, far != x)
+    passes = jnp.logical_and(speaks, jnp.logical_not(keeps))
     size = NC // PIECES
 
+    back_x = [(x + 2 - i) % 2 for i in range(2)]
+    back_z = [(z + 4 - i) % 4 for i in range(4)]
+    back_y = [(y + 4 - i) % 4 for i in range(4)]
+    part_x, part_z = [v * 16 for v in back_x], [v * 4 for v in back_z]
+
     def there(step):
-        return (x + step[0]) % 2 * 16 + (z + step[1]) % 4 * 4 + (y + step[2]) % 4
+        return part_x[-step[0] % 2] + part_z[-step[1] % 4] + back_y[-step[2] % 4]
 
     def source(offset):
         ox, oz, oy = split_offset(offset)
-        return (x - ox) % 2 * 16 + (z - oz) % 4 * 4 + (y - oy) % 4
+        return part_x[ox] + part_z[oz] + back_y[oy]
+
+    lines = [back_z[j] == y for j in range(4)]
+    serve_line = [jnp.logical_and(serves, v) for v in lines]
+    keep_line = [jnp.logical_and(keeps, v) for v in lines]
+    both_line = [jnp.logical_and(both, v) for v in lines]
+
+    load = pltpu.make_async_copy(x_ref, raw, local_sem)
+    load.start()
 
     barrier = pltpu.get_barrier_semaphore()
     for which, plan in enumerate(PLANS):
@@ -95,9 +113,13 @@
                 pl.semaphore_signal(barrier, inc=1, device_id={"row": there(behind), "col": col})
 
     pl.semaphore_signal(barrier, inc=1, device_id=peer)
-    pl.semaphore_signal(barrier, inc=1, device_id=other)
-
-    flat[...] = x_ref[...].reshape(DEPTH, NC).astype(jnp.float32)
+
+    @pl.when(passes)
+    def _():
+        pl.semaphore_signal(barrier, inc=1, device_id=server)
+
+    load.wait()
+    flat[...] = raw[...].reshape(DEPTH, NC).astype(jnp.float32)
     for c, bins in enumerate(CLASSES):
         tail = 8 * LANE + c // 4 * LANE + c % 4 * 16
         for part in range(2):
@@ -115,9 +137,10 @@
     keep = pltpu.make_async_copy(own, all_ref.at[row], local_sem)
     keep.start()
 
-    def first_copy(src, index, slot, piece, device):
+    def first_copy(src, index, slot, piece, which, device):
         return pltpu.make_async_remote_copy(
-            src_ref=src, dst_ref=first_ref.at[slot, pl.ds(piece * size, size)], send_sem=first_send.at[index],
+            src_ref=src, dst_ref=first_ref.at[slot, pl.ds(piece * size, size)],
+            send_sem=first_send.at[which * 4 * PIECES + index],
             recv_sem=first_recv.at[index], device_id=device,
         )
 
@@ -126,24 +149,35 @@
         return pltpu.make_async_copy(place, place, sem)
 
     def serve(piece, offset):
-        origin = source(offset)
+        ox, oz, oy = split_offset(offset)
         rows = pl.ds(piece * size, size)
-        src = own.at[rows] if offset == 0 else all_ref.at[origin, rows]
-        slot = origin % 4
+        src = own.at[rows] if offset == 0 else all_ref.at[source(offset), rows]
+        slot = back_y[oy]
         index = slot * PIECES + piece
-        wanted = origin // 4 == line
-
-        @pl.when(jnp.logical_and(wanted, passes))
-        def _():
-            first_copy(src, index, slot, piece, other).start()
-
-        @pl.when(jnp.logical_and(wanted, keeps))
-        def _():
-            first_copy(src, index, slot, piece, peer).start()
+
+        @pl.when(serve_line[oz])
+        def _():
+            first_copy(src, index, slot, piece, 0, target).start()
+
+        @pl.when(both_line[oz])
+        def _():
+            first_copy(src, index, slot, piece, 1, second).start()
+
+        @pl.when(keep_line[oz])
+        def _():
+            first_copy(src, index, slot, piece, 1, peer).start()
             pltpu.make_async_copy(src, first_ref.at[slot, rows], first_recv.at[index]).start()
 
+    def pass_on():
+        @pl.when(passes)
+        def _():
+            for index in range(4 * PIECES):
+                slot, piece = index // PIECES, index % PIECES
+                part(index, first_recv.at[index]).wait()
+                first_copy(first_ref.at[slot, pl.ds(piece * size, size)], index, slot, piece, 2, peer).start()
+
     def move(plan):
-        pl.semaphore_wait(barrier, len(steps_of(plan)) + 2)
+        pl.semaphore_wait(barrier, len(steps_of(plan)) + 1 + jnp.where(both, 2, jnp.where(keeps, 1, 0)))
         sent = []
         seen = set()
         for n, (step, piece, offset) in enumerate(plan):
@@ -163,8 +197,10 @@
                 )
                 copy.start()
                 sent.append(copy)
-            if fresh:
+            if fresh and offset < NR // 2:
                 serve(piece, offset)
+            if n == len(plan) - PASS_BEFORE:
+                pass_on()
         assert len(seen) == PIECES * NR and len(sent) == PIECES * (NR - 1)
         return sent
 
@@ -173,31 +209,23 @@
         @pl.when(core == which)
         def _():
             sent = move(plan)
-            for index in range(4 * PIECES):
-                part(index, first_recv.at[index]).wait()
-
-                @pl.when(passes)
-                def _():
-                    pltpu.make_async_remote_copy(
-                        src_ref=first_ref.at[index // PIECES, pl.ds(index % PIECES * size, size)],
-                        dst_ref=first_ref.at[index // PIECES, pl.ds(index % PIECES * size, size)],
-                        send_sem=first_send.at[4 * PIECES + index], recv_sem=first_recv.at[index], device_id=peer,
-                    ).start()
+
+            @pl.when(jnp.logical_not(passes))
+            def _():
+                for index in range(4 * PIECES):
+                    part(index, first_recv.at[index]).wait()
 
             for copy in sent:
                 copy.wait_send()
 
     keep.wait()
 
-    @pl.when(serves)
-    def _():
-        for index in range(4 * PIECES):
-            part(index, first_send.at[index]).wait()
-
-    @pl.when(passes)
-    def _():
-        for index in range(4 * PIECES):
-            part(index, first_send.at[4 * PIECES + index]).wait()
+    for which, taken in enumerate((serves, serves, passes)):
+
+        @pl.when(taken)
+        def _():
+            for index in range(4 * PIECES):
+                part(index, first_send.at[which * 4 * PIECES + index]).wait()
 
 
 def butterflies(zero, eight, real, imag):
@@ -284,8 +312,8 @@
         right = jnp.concatenate([all_ref[rows, main], all_ref[rows, tail]], axis=1)
         prod[c] = lax.dot_general(left[c], right, (((1,), (1,)), ((), ())), preferred_element_type=jnp.float32)
 
-    def combine(prod, slot, band):
-        for block in range(BAND // 8):
+    def combine(prod, slot, band, part):
+        for block in range(part * BAND // 32, (part + 1) * BAND // 32):
             start = pl.multiple_of(band * BAND + block * 8, 8)
             for lag in range(2):
                 for half in range(TILE // WIDE):
@@ -310,14 +338,13 @@
         multiply(prods[0], 0, c)
     for tile in range(tiles):
 
-        @pl.loop(0, bands)
-        def _(band):
+        for band in range(bands):
             if tile >= 2:
                 writes(tile - 2, band).wait()
-            if tile + 1 < tiles:
-                for i in range(8 // bands):
+            for i in range(8 // bands):
+                if tile + 1 < tiles:
                     multiply(prods[(tile + 1) % 2], tile + 1, band * (8 // bands) + i)
-            combine(prods[tile % 2], tile % 2, band)
+                combine(prods[tile % 2], tile % 2, band, i)
             writes(tile, band).start()
 
     for tile in range(max(tiles - 2, 0), tiles):
@@ -350,15 +377,16 @@
             jax.ShapeDtypeStruct((NR, NC, DEPTH), jnp.bfloat16),
             jax.ShapeDtypeStruct((4, NC, DEPTH), jnp.bfloat16),
         ),
-        in_specs=[pl.BlockSpec(memory_space=pltpu.VMEM)],
+        in_specs=[pl.BlockSpec(memory_space=pltpu.HBM)],
         out_specs=(pl.BlockSpec(memory_space=pl.ANY), pl.BlockSpec(memory_space=pl.ANY)),
         scratch_shapes=[
+            pltpu.VMEM((2, NW, NF, NC), jnp.bfloat16),
             pltpu.VMEM((DEPTH, NC), jnp.float32),
             pltpu.VMEM((DEPTH, NC), jnp.float32),
             pltpu.VMEM((NC, DEPTH), jnp.bfloat16),
             pltpu.SemaphoreType.DMA((PIECES * (NR - 1),)),
             pltpu.SemaphoreType.DMA((PIECES * NR,)),
-            pltpu.SemaphoreType.DMA((8 * PIECES,)),
+            pltpu.SemaphoreType.DMA((12 * PIECES,)),
             pltpu.SemaphoreType.DMA((4 * PIECES,)),
             pltpu.SemaphoreType.DMA,
         ],
@@ -366,7 +394,7 @@
             collective_id=0, has_side_effects=True, vmem_limit_bytes=16 * 1024 * 1024
         ),
         name="gather",
-    )(spectra)
+    )(pltpu.with_memory_space_constraint(spectra, pltpu.HBM))
     return product_call(first.reshape(4 * NC, DEPTH), gathered.reshape(NR * NC, DEPTH))
 
 

time: 35.6 us -> 33 us (0.927); the launches traced: 35.1 us -> 32.9 us
  Pallas kernels: 34.1 us -> 32.9 us
  local copies, waits for them, and re-layouts: 0.97 us -> 0 us
    unnamed x2 -> x0, local copies, waits for them, and re-layouts: 0.97 us -> none
    pallas_call x1, Pallas kernels: 26.4 us -> 25.6 us  [on_device(): pl.pallas_call(gather_kernel, out_shape=(jax.ShapeDtypeStruct((NR, NC, DE...]
    pallas_call x1, Pallas kernels: 7.7 us -> 7.24 us  [product_call(): pl.pallas_call(product_kernel, out_shape=jax.ShapeDtypeStruct((NF, 4 * NC...]
where the time goes in v3:
time: 33 us; the launch traced here: 32.9 us
  Pallas kernels  32.9 us (100%)
    pallas_call x1, Pallas kernels, on_device(): pl.pallas_call(gather_kernel, out_shape=(jax.ShapeDtypeStruct((NR, NC, DE...  25.6 us
    pallas_call x1, Pallas kernels, product_call(): pl.pallas_call(product_kernel, out_shape=jax.ShapeDtypeStruct((NF, 4 * NC...  7.24 us

profile of v3, /device:TPU:35, one launch (start us, length us, event | category | flops | bytes accessed | tf_op | source)
XLA Modules:
  0.0 32.9 jit_solution(14963095783745058771)
XLA Ops:
  0.0 25.6 %gather.1 = (bf16[32,32,1280]{2,1,0:T(8,128)(2,1)S(1)}, bf16[4,32,1280]{2,1,0:T(8,128)(2,1)S(1)}) custom-call(bf16[2,20,32,32]{3,2,1,0:T(8,128)(2,1)} %x_ref.1), custom_call_target="tpu_custom_call" | custom-call | tf_op jit(solution)/shard_map/gather/pallas_call | solution.py:374
  25.7 7.2 %product.1 = f32[32,128,1024]{2,1,0:T(8,128)} custom-call(bf16[128,1280]{1,0:T(8,128)(2,1)S(1)} %bitcast.3, bf16[1024,1280]{1,0:T(8,128)(2,1)S(1)} %bitcast.2), custom_call_target="tpu_custom_call" | custom-call | tf_op jit(solution)/shard_map/product/pallas_call | solution.py:356

commit v4 on v3

--- a/solution.py
+++ b/solution.py
@@ -47,7 +47,13 @@
     (1, 0, 0), (0, 0, 1), (0, 0, 3), (0, 1, 0), (0, 3, 0), (0, 0, 2), (0, 1, 1), (0, 2, 0),
     (0, 3, 1),
 )
-PASS_BEFORE = 8
+PASS_BEFORE = 14
+
+
+def ends_of(plan):
+    onward = {entry[1:] for entry in plan if entry[0] >= 0}
+    every = {(piece, offset) for piece in range(PIECES) for offset in range(NR // 2, NR)}
+    return every - onward
 
 
 def steps_of(plan):
@@ -97,8 +103,6 @@
 
     lines = [back_z[j] == y for j in range(4)]
     serve_line = [jnp.logical_and(serves, v) for v in lines]
-    keep_line = [jnp.logical_and(keeps, v) for v in lines]
-    both_line = [jnp.logical_and(both, v) for v in lines]
 
     load = pltpu.make_async_copy(x_ref, raw, local_sem)
     load.start()
@@ -137,50 +141,48 @@
     keep = pltpu.make_async_copy(own, all_ref.at[row], local_sem)
     keep.start()
 
-    def first_copy(src, index, slot, piece, which, device):
+    def first_copy(src, dst, which, device):
         return pltpu.make_async_remote_copy(
-            src_ref=src, dst_ref=first_ref.at[slot, pl.ds(piece * size, size)],
-            send_sem=first_send.at[which * 4 * PIECES + index],
-            recv_sem=first_recv.at[index], device_id=device,
+            src_ref=src, dst_ref=dst, send_sem=first_send.at[which], recv_sem=first_recv, device_id=device
         )
 
-    def part(index, sem):
-        place = first_ref.at[index // PIECES, pl.ds(index % PIECES * size, size)]
-        return pltpu.make_async_copy(place, place, sem)
+    def all_firsts(sem):
+        pltpu.make_async_copy(first_ref, first_ref, sem).wait()
 
     def serve(piece, offset):
         ox, oz, oy = split_offset(offset)
         rows = pl.ds(piece * size, size)
         src = own.at[rows] if offset == 0 else all_ref.at[source(offset), rows]
-        slot = back_y[oy]
-        index = slot * PIECES + piece
+        dst = first_ref.at[back_y[oy], rows]
 
         @pl.when(serve_line[oz])
         def _():
-            first_copy(src, index, slot, piece, 0, target).start()
-
-        @pl.when(both_line[oz])
-        def _():
-            first_copy(src, index, slot, piece, 1, second).start()
-
-        @pl.when(keep_line[oz])
-        def _():
-            first_copy(src, index, slot, piece, 1, peer).start()
-            pltpu.make_async_copy(src, first_ref.at[slot, rows], first_recv.at[index]).start()
+            first_copy(src, dst, 0, target).start()
+
+            @pl.when(both)
+            def _():
+                first_copy(src, dst, 1, second).start()
+
+            @pl.when(keeps)
+            def _():
+                first_copy(src, dst, 1, peer).start()
+                pltpu.make_async_copy(src, dst, first_recv).start()
 
     def pass_on():
         @pl.when(passes)
         def _():
-            for index in range(4 * PIECES):
-                slot, piece = index // PIECES, index % PIECES
-                part(index, first_recv.at[index]).wait()
-                first_copy(first_ref.at[slot, pl.ds(piece * size, size)], index, slot, piece, 2, peer).start()
+            all_firsts(first_recv)
+            first_copy(first_ref, first_ref, 2, peer).start()
 
     def move(plan):
         pl.semaphore_wait(barrier, len(steps_of(plan)) + 1 + jnp.where(both, 2, jnp.where(keeps, 1, 0)))
-        sent = []
+        late = ends_of(plan)
         seen = set()
         for n, (step, piece, offset) in enumerate(plan):
+            if n == len(plan) - PASS_BEFORE:
+                pass_on()
+            if (piece, offset) in late:
+                continue
             rows = pl.ds(piece * size, size)
             place = all_ref.at[source(offset), rows]
             fresh = (piece, offset) not in seen
@@ -188,44 +190,41 @@
             if fresh and offset:
                 pltpu.make_async_copy(place, place, recv_sem.at[piece * NR + offset]).wait()
             if step >= 0:
-                copy = pltpu.make_async_remote_copy(
+                to = (piece, shifted(offset, STEPS[step]))
+                pltpu.make_async_remote_copy(
                     src_ref=own.at[rows] if offset == 0 else place,
                     dst_ref=place,
-                    send_sem=send_sem.at[len(sent)],
-                    recv_sem=recv_sem.at[piece * NR + shifted(offset, STEPS[step])],
+                    send_sem=send_sem,
+                    recv_sem=recv_sem.at[piece * NR + (0 if to in late else to[1])],
                     device_id={"row": there(STEPS[step]), "col": col},
-                )
-                copy.start()
-                sent.append(copy)
+                ).start()
             if fresh and offset < NR // 2:
                 serve(piece, offset)
-            if n == len(plan) - PASS_BEFORE:
-                pass_on()
-        assert len(seen) == PIECES * NR and len(sent) == PIECES * (NR - 1)
-        return sent
+        assert len(seen) + len(late) == PIECES * NR
+        for piece in range(PIECES):
+            count = sum(1 for entry in late if entry[0] == piece)
+            place = all_ref.at[pl.ds(0, count), pl.ds(piece * size, size)]
+            pltpu.make_async_copy(place, place, recv_sem.at[piece * NR]).wait()
 
     for which, plan in enumerate(PLANS):
 
         @pl.when(core == which)
         def _():
-            sent = move(plan)
-
-            @pl.when(jnp.logical_not(passes))
-            def _():
-                for index in range(4 * PIECES):
-                    part(index, first_recv.at[index]).wait()
-
-            for copy in sent:
-                copy.wait_send()
-
+            move(plan)
+
+    @pl.when(jnp.logical_not(passes))
+    def _():
+        all_firsts(first_recv)
+
+    place = all_ref.at[pl.ds(0, NR - 1)]
+    pltpu.make_async_copy(place, place, send_sem).wait()
     keep.wait()
 
     for which, taken in enumerate((serves, serves, passes)):
 
         @pl.when(taken)
         def _():
-            for index in range(4 * PIECES):
-                part(index, first_send.at[which * 4 * PIECES + index]).wait()
+            all_firsts(first_send.at[which])
 
 
 def butterflies(zero, eight, real, imag):
@@ -384,10 +383,10 @@
             pltpu.VMEM((DEPTH, NC), jnp.float32),
             pltpu.VMEM((DEPTH, NC), jnp.float32),
             pltpu.VMEM((NC, DEPTH), jnp.bfloat16),
-            pltpu.SemaphoreType.DMA((PIECES * (NR - 1),)),
+            pltpu.SemaphoreType.DMA,
             pltpu.SemaphoreType.DMA((PIECES * NR,)),
-            pltpu.SemaphoreType.DMA((12 * PIECES,)),
-            pltpu.SemaphoreType.DMA((4 * PIECES,)),
+            pltpu.SemaphoreType.DMA((3,)),
+            pltpu.SemaphoreType.DMA,
             pltpu.SemaphoreType.DMA,
         ],
         compiler_params=pltpu.CompilerParams(

time: 33 us -> 32.4 us (0.982)
  Pallas kernels: 32.9 us -> 32.3 us
    pallas_call x1, Pallas kernels: 25.6 us -> 25 us  [on_device(): pl.pallas_call(gather_kernel, out_shape=(jax.ShapeDtypeStruct((NR, NC, DE...]
where the time goes in v4:
time: 32.4 us; the launch traced here: 32.3 us
  Pallas kernels  32.3 us (100%)
    pallas_call x1, Pallas kernels, on_device(): pl.pallas_call(gather_kernel, out_shape=(jax.ShapeDtypeStruct((NR, NC, DE...  25 us
    pallas_call x1, Pallas kernels, product_call(): pl.pallas_call(product_kernel, out_shape=jax.ShapeDtypeStruct((NF, 4 * NC...  7.24 us

profile of v4, /device:TPU:35, one launch (start us, length us, event | category | flops | bytes accessed | tf_op | source)
XLA Modules:
  0.0 32.3 jit_solution(10825442928400631712)
XLA Ops:
  0.0 25.0 %gather.1 = (bf16[32,32,1280]{2,1,0:T(8,128)(2,1)S(1)}, bf16[4,32,1280]{2,1,0:T(8,128)(2,1)S(1)}) custom-call(bf16[2,20,32,32]{3,2,1,0:T(8,128)(2,1)} %x_ref.1), custom_call_target="tpu_custom_call" | custom-call | tf_op jit(solution)/shard_map/gather/pallas_call | solution.py:373
  25.0 7.2 %product.1 = f32[32,128,1024]{2,1,0:T(8,128)} custom-call(bf16[128,1280]{1,0:T(8,128)(2,1)S(1)} %bitcast.3, bf16[1024,1280]{1,0:T(8,128)(2,1)S(1)} %bitcast.2), custom_call_target="tpu_custom_call" | custom-call | tf_op jit(solution)/shard_map/product/pallas_call | solution.py:355

commit v5 on v4

--- a/solution.py
+++ b/solution.py
@@ -14,38 +14,37 @@
 SCALE = 1.0 / math.sqrt(float(DEPTH))
 
 PLAN_0 = (
-    (1, 1, 0), (3, 1, 0), (4, 1, 0), (0, 0, 0), (2, 1, 0), (2, 0, 0), (0, 1, 0), (6, 0, 0),
-    (1, 0, 0), (3, 0, 0), (4, 0, 0), (7, 1, 1), (1, 1, 1), (0, 1, 4), (3, 1, 4), (1, 1, 12),
-    (2, 1, 12), (0, 1, 3), (1, 0, 16), (4, 0, 1), (3, 0, 5), (2, 0, 4), (0, 0, 5), (4, 0, 12),
-    (1, 0, 5), (3, 0, 16), (2, 0, 12), (0, 1, 1), (4, 0, 16), (2, 0, 3), (1, 1, 4), (2, 0, 16),
-    (2, 1, 4), (0, 1, 12), (4, 1, 2), (3, 1, 2), (1, 1, 9), (0, 1, 9), (-1, 1, 8), (4, 1, 15),
-    (3, 1, 20), (1, 0, 13), (2, 1, 19), (1, 0, 9), (3, 0, 7), (0, 0, 8), (-1, 0, 6), (-1, 1, 13),
-    (1, 0, 21), (0, 0, 15), (2, 1, 20), (-1, 1, 5), (4, 1, 19), (-1, 0, 2), (6, 1, 17), (0, 1, 14),
-    (0, 1, 10), (4, 1, 17), (2, 1, 24), (-1, 1, 11), (-1, 1, 7), (1, 1, 20), (0, 0, 14), (-1, 0, 11),
-    (-1, 1, 6), (3, 0, 21), (4, 0, 17), (-1, 0, 10), (2, 0, 20), (1, 0, 17), (3, 0, 22), (2, 0, 24),
-    (-1, 1, 22), (-1, 1, 25), (-1, 1, 23), (-1, 1, 29), (-1, 0, 31), (-1, 0, 19), (-1, 1, 27), (-1, 1, 28),
-    (-1, 0, 28), (-1, 1, 26), (-1, 1, 30), (-1, 1, 31), (-1, 0, 25), (-1, 1, 16), (-1, 1, 21), (-1, 1, 18),
-    (-1, 0, 23), (-1, 0, 29), (-1, 0, 18), (-1, 0, 30), (-1, 0, 26), (-1, 0, 27),
+    (5, 0, 0), (4, 1, 0), (1, 0, 0), (2, 0, 0), (0, 0, 0), (3, 0, 0), (2, 1, 0), (5, 1, 0),
+    (0, 1, 0), (1, 1, 0), (4, 0, 0), (4, 1, 12), (0, 1, 12), (3, 0, 3), (5, 0, 5), (0, 0, 3),
+    (2, 0, 12), (4, 0, 12), (1, 0, 12), (2, 1, 3), (4, 0, 16), (0, 0, 5), (2, 1, 16), (1, 1, 5),
+    (3, 1, 5), (3, 0, 16), (1, 0, 5), (1, 0, 1), (2, 1, 12), (0, 1, 1), (4, 1, 1), (3, 1, 3),
+    (-1, 0, 4), (3, 0, 5), (0, 1, 5), (4, 1, 8), (2, 1, 8), (2, 1, 28), (4, 0, 15), (-1, 0, 8),
+    (1, 0, 13), (-1, 0, 7), (0, 0, 10), (4, 1, 2), (1, 0, 16), (3, 1, 6), (4, 1, 28), (1, 0, 28),
+    (2, 0, 28), (0, 1, 9), (3, 1, 16), (4, 0, 28), (-1, 1, 13), (0, 0, 6), (1, 1, 17), (2, 0, 20),
+    (-1, 1, 15), (3, 0, 21), (-1, 1, 4), (3, 1, 19), (-1, 0, 2), (-1, 1, 11), (-1, 1, 7), (4, 1, 17),
+    (2, 0, 19), (1, 1, 21), (-1, 0, 9), (-1, 0, 11), (-1, 0, 14), (4, 1, 31), (2, 1, 31), (-1, 1, 14),
+    (1, 0, 26), (3, 0, 26), (0, 1, 10), (-1, 1, 20), (-1, 0, 24), (-1, 0, 22), (-1, 1, 25), (-1, 0, 31),
+    (-1, 0, 29), (-1, 0, 25), (-1, 1, 22), (-1, 1, 18), (-1, 1, 23), (-1, 1, 29), (-1, 0, 17), (-1, 0, 18),
+    (-1, 1, 30), (-1, 1, 24), (-1, 1, 27), (-1, 0, 23), (-1, 0, 27), (-1, 0, 30), (-1, 1, 26),
 )
 PLAN_1 = (
-    (4, 1, 0), (3, 1, 0), (0, 0, 0), (5, 1, 0), (5, 0, 0), (1, 0, 0), (0, 1, 0), (3, 0, 0),
-    (4, 0, 0), (3, 1, 4), (2, 1, 4), (0, 1, 12), (8, 1, 12), (2, 1, 12), (3, 0, 16), (3, 0, 4),
-    (0, 1, 4), (1, 0, 12), (4, 0, 16), (2, 0, 4), (0, 1, 2), (4, 1, 2), (1, 1, 16), (2, 1, 2),
-    (1, 1, 12), (3, 0, 2), (0, 0, 2), (3, 0, 1), (4, 0, 2), (2, 1, 7), (0, 1, 7), (-1, 1, 8),
-    (3, 1, 7), (8, 1, 28), (3, 0, 20), (0, 1, 15), (1, 1, 9), (2, 0, 8), (4, 0, 13), (2, 1, 16),
-    (2, 1, 0), (2, 0, 20), (1, 1, 28), (0, 0, 13), (1, 0, 20), (3, 0, 6), (4, 1, 9), (1, 1, 20),
-    (0, 1, 14), (4, 0, 7), (3, 0, 18), (4, 1, 28), (1, 0, 18), (-1, 1, 11), (4, 0, 18), (0, 1, 6),
-    (3, 0, 11), (-1, 1, 10), (2, 0, 18), (1, 0, 24), (-1, 0, 5), (-1, 0, 9), (2, 0, 24), (3, 1, 23),
-    (0, 0, 10), (-1, 1, 5), (-1, 1, 1), (-1, 1, 13), (1, 1, 25), (2, 0, 28), (-1, 1, 3), (-1, 1, 18),
-    (-1, 0, 14), (-1, 0, 3), (-1, 1, 31), (-1, 1, 30), (-1, 0, 22), (-1, 0, 15), (-1, 0, 21), (-1, 1, 29),
-    (-1, 1, 24), (-1, 0, 23), (-1, 0, 19), (-1, 0, 29), (-1, 1, 21), (-1, 0, 17), (-1, 1, 22), (-1, 0, 25),
-    (-1, 1, 19), (-1, 0, 30), (-1, 0, 27), (-1, 1, 27), (-1, 1, 17), (-1, 0, 26), (-1, 1, 26), (-1, 0, 31),
+    (5, 1, 0), (2, 1, 0), (3, 1, 0), (6, 1, 0), (4, 0, 0), (5, 0, 0), (1, 0, 0), (0, 0, 0),
+    (1, 1, 0), (2, 0, 0), (0, 1, 0), (4, 1, 3), (3, 0, 0), (2, 1, 3), (0, 1, 3), (3, 1, 5),
+    (1, 1, 5), (4, 0, 3), (2, 1, 28), (1, 0, 16), (3, 0, 5), (4, 0, 12), (0, 1, 5), (2, 0, 16),
+    (1, 0, 1), (3, 1, 3), (1, 0, 5), (3, 1, 4), (4, 1, 15), (2, 1, 15), (-1, 0, 4), (3, 0, 3),
+    (4, 1, 1), (1, 1, 28), (2, 0, 15), (0, 1, 9), (2, 1, 19), (3, 0, 16), (4, 0, 15), (3, 1, 6),
+    (4, 0, 1), (0, 0, 8), (1, 0, 9), (4, 0, 16), (4, 0, 17), (2, 0, 19), (1, 1, 21), (-1, 1, 2),
+    (-1, 1, 7), (0, 1, 11), (2, 1, 21), (1, 1, 16), (-1, 1, 14), (0, 0, 6), (2, 1, 31), (-1, 0, 2),
+    (3, 1, 8), (-1, 1, 13), (3, 1, 19), (-1, 0, 14), (4, 0, 19), (3, 0, 19), (2, 1, 25), (-1, 0, 7),
+    (0, 0, 11), (1, 0, 24), (0, 0, 10), (1, 0, 20), (-1, 0, 13), (4, 0, 18), (2, 1, 27), (-1, 1, 10),
+    (-1, 1, 12), (-1, 1, 30), (-1, 1, 18), (-1, 1, 23), (-1, 1, 17), (-1, 0, 27), (-1, 0, 31), (-1, 1, 20),
+    (-1, 1, 24), (-1, 1, 22), (-1, 0, 22), (-1, 0, 29), (-1, 1, 29), (-1, 0, 25), (-1, 0, 28), (-1, 0, 23),
+    (-1, 0, 21), (-1, 0, 26), (-1, 0, 30), (-1, 1, 26),
 )
 PLANS = (PLAN_0, PLAN_1)
 PIECES = 2
 STEPS = (
-    (1, 0, 0), (0, 0, 1), (0, 0, 3), (0, 1, 0), (0, 3, 0), (0, 0, 2), (0, 1, 1), (0, 2, 0),
-    (0, 3, 1),
+    (1, 0, 0), (0, 0, 1), (0, 0, 3), (0, 1, 0), (0, 3, 0), (0, 1, 1), (1, 3, 0),
 )
 PASS_BEFORE = 14
 

time: 32.4 us -> 31.7 us (0.978)
  Pallas kernels: 32.3 us -> 31.5 us
    pallas_call x1, Pallas kernels: 25 us -> 24.3 us  [on_device(): pl.pallas_call(gather_kernel, out_shape=(jax.ShapeDtypeStruct((NR, NC, DE...]
where the time goes in v5:
time: 31.7 us; the launch traced here: 31.5 us
  Pallas kernels  31.5 us (99%)
    pallas_call x1, Pallas kernels, on_device(): pl.pallas_call(gather_kernel, out_shape=(jax.ShapeDtypeStruct((NR, NC, DE...  24.3 us
    pallas_call x1, Pallas kernels, product_call(): pl.pallas_call(product_kernel, out_shape=jax.ShapeDtypeStruct((NF, 4 * NC...  7.24 us

profile of v5, /device:TPU:35, one launch (start us, length us, event | category | flops | bytes accessed | tf_op | source)
XLA Modules:
  0.0 31.5 jit_solution(10603795108910803996)
XLA Ops:
  0.0 24.3 %gather.1 = (bf16[32,32,1280]{2,1,0:T(8,128)(2,1)S(1)}, bf16[4,32,1280]{2,1,0:T(8,128)(2,1)S(1)}) custom-call(bf16[2,20,32,32]{3,2,1,0:T(8,128)(2,1)} %x_ref.1), custom_call_target="tpu_custom_call" | custom-call | tf_op jit(solution)/shard_map/gather/pallas_call | solution.py:372
  24.3 7.2 %product.1 = f32[32,128,1024]{2,1,0:T(8,128)} custom-call(bf16[128,1280]{1,0:T(8,128)(2,1)S(1)} %bitcast.3, bf16[1024,1280]{1,0:T(8,128)(2,1)S(1)} %bitcast.2), custom_call_target="tpu_custom_call" | custom-call | tf_op jit(solution)/shard_map/product/pallas_call | solution.py:354

commit v6 on v5

--- a/solution.py
+++ b/solution.py
@@ -122,7 +122,7 @@
         pl.semaphore_signal(barrier, inc=1, device_id=server)
 
     load.wait()
-    flat[...] = raw[...].reshape(DEPTH, NC).astype(jnp.float32)
+    flat[:DEPTH, :] = raw[...].reshape(DEPTH, NC).astype(jnp.float32)
     for c, bins in enumerate(CLASSES):
         tail = 8 * LANE + c // 4 * LANE + c % 4 * 16
         for part in range(2):
@@ -379,7 +379,7 @@
         out_specs=(pl.BlockSpec(memory_space=pl.ANY), pl.BlockSpec(memory_space=pl.ANY)),
         scratch_shapes=[
             pltpu.VMEM((2, NW, NF, NC), jnp.bfloat16),
-            pltpu.VMEM((DEPTH, NC), jnp.float32),
+            pltpu.VMEM((DEPTH + 5 * NF, NC), jnp.float32),
             pltpu.VMEM((DEPTH, NC), jnp.float32),
             pltpu.VMEM((NC, DEPTH), jnp.bfloat16),
             pltpu.SemaphoreType.DMA,

time: 31.7 us -> 31.7 us (level)
  no operation moved by 1% of the time
where the time goes in v6:
time: 31.7 us; the launch traced here: 31.5 us
  Pallas kernels  31.5 us (99%)
    pallas_call x1, Pallas kernels, on_device(): pl.pallas_call(gather_kernel, out_shape=(jax.ShapeDtypeStruct((NR, NC, DE...  24.3 us
    pallas_call x1, Pallas kernels, product_call(): pl.pallas_call(product_kernel, out_shape=jax.ShapeDtypeStruct((NF, 4 * NC...  7.24 us

profile of v6, /device:TPU:35, one launch (start us, length us, event | category | flops | bytes accessed | tf_op | source)
XLA Modules:
  0.0 31.5 jit_solution(5365756523593698704)
XLA Ops:
  0.0 24.3 %gather.1 = (bf16[32,32,1280]{2,1,0:T(8,128)(2,1)S(1)}, bf16[4,32,1280]{2,1,0:T(8,128)(2,1)S(1)}) custom-call(bf16[2,20,32,32]{3,2,1,0:T(8,128)(2,1)} %x_ref.1), custom_call_target="tpu_custom_call" | custom-call | tf_op jit(solution)/shard_map/gather/pallas_call | solution.py:372
  24.3 7.2 %product.1 = f32[32,128,1024]{2,1,0:T(8,128)} custom-call(bf16[128,1280]{1,0:T(8,128)(2,1)S(1)} %bitcast.3, bf16[1024,1280]{1,0:T(8,128)(2,1)S(1)} %bitcast.2), custom_call_target="tpu_custom_call" | custom-call | tf_op jit(solution)/shard_map/product/pallas_call | solution.py:354
